TPU v7x, 32 devices: a whole 2x2x4 slice. The times are simulated.
32 devices in a mesh: row: 4 (over z), col: 8 (over y, x, core).
Axes of the slice: x: 2, y: 2, z: 4, core: 2. Of those that a mesh axis runs over, the one named last changes fastest.
Arguments:
- momentum: float32 [16384, 16384], P('row', 'col'), may hold values from -18 to 18
- gradient: bfloat16 [16384, 16384], P('row', 'col'), may hold values from -6 to 6
- right_factor: float32 [16384, 64], P('col'), may hold values from -1 to 1
Outputs:
- update: bfloat16 [16384, 16384], P('row', 'col')
- left: float32 [16384, 64], P('row')
- normed: float32 [16384, 64], P('col')
- new_momentum: float32 [16384, 16384], P('row', 'col')
- first_factor: float32 [64, 64], replicated
All inputs are finite; a program needn't handle non-finite values.
Results may differ from a plain program's by a relative error of at most 0.001.
Values sent between devices are 32-bit elements; how exact they have to be, the bound alone decides.
A program may use at most 192 MiB of HBM per device.

v0:
```python
import jax
import jax.numpy as jnp
from jax import lax
from jax.sharding import PartitionSpec as P

NROW = 16384
NCOL = 16384
RANK = 64


HIGH = lax.Precision.HIGHEST


def gram_of(block):
    return jnp.dot(block.T, block, precision=HIGH, preferred_element_type=jnp.float32)


def apply_lower(block, lower):
    return lax.linalg.triangular_solve(lower, block, left_side=False, lower=True, transpose_a=True)


def right_part(blended, factor):
    return lax.dot_general(
        blended,
        factor,
        (((0,), (0,)), ((), ())),
        precision=HIGH,
        preferred_element_type=jnp.float32,
    )


def on_device(momentum, gradient, right_factor):
    blended = momentum + gradient.astype(jnp.float32)
    partial_value = jnp.dot(
        blended, right_factor, precision=HIGH, preferred_element_type=jnp.float32
    )
    left_raw = lax.psum(partial_value, "col")
    gram_one = lax.psum(gram_of(left_raw), "row")
    lower_one = jnp.linalg.cholesky(gram_one)
    left_one = apply_lower(left_raw, lower_one)
    first_factor = lower_one / jnp.sqrt(jnp.float32(NROW) * jnp.float32(NCOL))
    gram_two = lax.psum(gram_of(left_one), "row")
    lower_two = jnp.linalg.cholesky(gram_two)
    left = apply_lower(left_one, lower_two)
    right = lax.psum(right_part(blended, left), "row")
    squares = lax.psum(jnp.sum(right * right, axis=0), "col")
    normed = right / (jnp.sqrt(squares) + 1e-06)
    scale = jnp.sqrt(jnp.float32(NROW) * jnp.float32(NCOL) / jnp.float32(RANK))
    update = (
        scale * jnp.dot(left, normed.T, precision=HIGH, preferred_element_type=jnp.float32)
    ).astype(jnp.bfloat16)
    new_momentum = blended - 0.05 * jnp.dot(
        left, right.T, precision=HIGH, preferred_element_type=jnp.float32
    )
    return (update, left, normed, new_momentum, first_factor)


def solution(mesh):
    in_specs = (P("row", "col"), P("row", "col"), P("col", None))
    out_specs = (P("row", "col"), P("row", None), P("col", None), P("row", "col"), P())
    return jax.shard_map(
        on_device, mesh=mesh, in_specs=in_specs, out_specs=out_specs, check_vma=False
    )
```

profile of v0, /device:TPU:0, one launch (start us, length us, event | category | flops | bytes accessed | tf_op | source)
XLA Modules:
  0.0 329.2 jit_solution(17077890868684649098)
XLA Ops:
  7.2 0.0 copy-start
  7.2 0.0 all-reduce.3.cloned.1.call-start
  7.2 1.0 copy-done
  8.2 40.1 %fusion.1 = f32[4096,64]{0,1:T(8,128)} fusion(f32[2048,64]{0,1:T(8,128)S(1)} %copy-done, f32[4096,2048]{1,0:T(8,128)} %param.6, bf16[4096,2048]{1,0:T(8,128)(2,1)} %param.7), kind=kOutput, calls=%fused_computation.4 | convolution fusion | flops 6459228160 | bytes 51904512 | tf_op jit(solution)/shard_map/dot_general | solution.py:34
  48.3 0.0 all-reduce.3.cloned.1.call-update
  48.4 0.0 all-reduce.5.cloned.1.call-start
  48.4 59.4 %all-reduce.3.cloned.1.call-done = f32[4096,64]{0,1:T(8,128)} async-done(((f32[4096,64]{0,1:T(8,128)}), f32[4096,64]{0,1:T(8,128)}) %all-reduce.3.cloned.1.call-update) | async-done | bytes 1048592 | tf_op jit(solution)/shard_map/psum | solution.py:37
  107.8 2.5 fusion.13
  110.3 18.8 %psum.36 = f32[64,64]{0,1:T(8,128)S(1)} all-reduce(f32[64,64]{0,1:T(8,128)S(1)} %fusion.13), channel_id=1, replica_groups=mesh['row'=4,'col'=8] {'row'}, use_global_device_ids=true, to_apply=%region_1.0 | all-reduce | flops 4096 | bytes 32768 | tf_op jit(solution)/shard_map/psum | solution.py:38
  129.2 0.1 copy.9
  129.3 5.8 %cholesky.44 = f32[64,64]{1,0:T(8,128)S(1)} custom-call(f32[64,64]{1,0:T(8,128)S(1)} %fusion.6), custom_call_target="Cholesky" | custom-call | tf_op jit(solution)/shard_map/jit(cholesky)/cholesky | solution.py:39
  135.2 0.6 compare_reduce_fusion.1
  135.8 1.3 fusion.12
  137.1 4.9 %custom-call.6 = f32[1,64,64]{1,2,0:T(8,128)S(1)} custom-call(f32[1,64,64]{2,1,0:T(8,128)S(1)} %get-tuple-element.8), custom_call_target="InvertDiagBlocksLowerTriangular" | custom-call | tf_op jit(solution)/shard_map/triangular_solve/custom-call.0 | solution.py:19
  142.0 2.3 convolution_bitcast_fusion.1
  144.2 1.0 fusion.14
  145.2 15.8 %psum.37 = f32[64,64]{0,1:T(8,128)S(1)} all-reduce(f32[64,64]{0,1:T(8,128)S(1)} %fusion.14), channel_id=1, replica_groups=mesh['row'=4,'col'=8] {'row'}, use_global_device_ids=true, to_apply=%region_4.7 | all-reduce | flops 4096 | bytes 32768 | tf_op jit(solution)/shard_map/psum | solution.py:42
  161.1 0.1 copy.11
  161.2 5.8 %cholesky.55 = f32[64,64]{1,0:T(8,128)S(1)} custom-call(f32[64,64]{1,0:T(8,128)S(1)} %fusion.4), custom_call_target="Cholesky" | custom-call | tf_op jit(solution)/shard_map/jit(cholesky)/cholesky | solution.py:43
  167.1 0.6 compare_reduce_fusion
  167.7 0.7 fusion.2
  168.4 4.9 %custom-call.7 = f32[1,64,64]{1,2,0:T(8,128)S(1)} custom-call(f32[1,64,64]{2,1,0:T(8,128)S(1)} %fusion.2), custom_call_target="InvertDiagBlocksLowerTriangular" | custom-call | tf_op jit(solution)/shard_map/triangular_solve/custom-call.0 | solution.py:19
  173.3 1.0 convolution_bitcast_fusion
  174.3 0.0 copy-start.2
  174.3 29.1 %fusion = f32[2048,64]{0,1:T(8,128)} fusion(f32[4096,64]{0,1:T(8,128)S(1)} %convolution_bitcast_fusion, f32[4096,2048]{1,0:T(8,128)} %param.6, bf16[4096,2048]{1,0:T(8,128)(2,1)} %param.7), kind=kOutput, calls=%fused_computation.3 | convolution fusion | flops 6459228160 | bytes 51904512 | tf_op jit(solution)/shard_map/dot_general | solution.py:23
  203.5 0.0 all-reduce.5.cloned.1.call-update
  203.5 36.1 %all-reduce.5.cloned.1.call-done = f32[2048,64]{0,1:T(8,128)} async-done(((f32[2048,64]{0,1:T(8,128)}), f32[2048,64]{0,1:T(8,128)}) %all-reduce.5.cloned.1.call-update) | async-done | bytes 524304 | tf_op jit(solution)/shard_map/psum | solution.py:45
  239.5 1.2 multiply_reduce_fusion
  240.7 13.1 %psum.39 = f32[64]{0:T(128)S(1)} all-reduce(f32[64]{0:T(128)S(1)} %multiply_reduce_fusion), channel_id=1, replica_groups=mesh['row'=4,'col'=8] {'col'}, use_global_device_ids=true, to_apply=%region_7.10 | all-reduce | flops 64 | bytes 512 | tf_op jit(solution)/shard_map/psum | solution.py:46
  253.9 1.2 broadcast_divide_fusion
  255.0 0.0 copy-start.3
  255.0 0.0 copy-start.1
  255.1 29.4 %multiply_convert_fusion = bf16[4096,2048]{1,0:T(8,128)(2,1)} fusion(f32[4096,64]{0,1:T(8,128)S(1)} %convolution_bitcast_fusion, f32[2048,64]{0,1:T(8,128)S(1)} %broadcast_divide_fusion), kind=kOutput, calls=%fused_computation.1 | convolution fusion | flops 6459228160 | bytes 18350080 | tf_op jit(solution)/shard_map/dot_general | solution.py:50
  284.4 0.0 copy-done.2
  284.4 37.9 %multiply_subtract_fusion = f32[4096,2048]{1,0:T(8,128)} fusion(f32[4096,64]{0,1:T(8,128)S(1)} %convolution_bitcast_fusion, f32[2048,64]{0,1:T(8,128)} %all-reduce.5.cloned.1.call-done, f32[4096,2048]{1,0:T(8,128)} %param.6, bf16[4096,2048]{1,0:T(8,128)(2,1)} %param.7), kind=kOutput, calls=%fused_computation | convolution fusion | flops 6476005376 | bytes 85458944 | tf_op jit(solution)/shard_map/dot_general | solution.py:52
  322.4 0.0 copy-done.3
  322.4 0.0 copy-done.1
  (5 shorter events, 0.1 us)
Async XLA Ops:
  7.2 1.1 copy-start
  7.2 100.6 %all-reduce.3.cloned.1.call-start = ((), (), s32[]{:S(2)}) async-start(), calls=%async_computation | async-start | bytes 2097152 | tf_op jit(solution)/shard_map/psum | solution.py:37
  48.4 191.2 %all-reduce.5.cloned.1.call-start = ((), (), s32[]{:S(2)}) async-start(), calls=%async_computation.1 | async-start | bytes 1048576 | tf_op jit(solution)/shard_map/psum | solution.py:45
  174.3 110.1 %copy-start.2 = (f32[4096,64]{0,1:T(8,128)}, f32[4096,64]{0,1:T(8,128)S(1)}, u32[]{:S(2)}) copy-start(f32[4096,64]{0,1:T(8,128)S(1)} %convolution_bitcast_fusion) | copy-start | bytes 3145732
  255.0 67.3 %copy-start.3 = (f32[2048,64]{0,1:T(8,128)}, f32[2048,64]{0,1:T(8,128)S(1)}, u32[]{:S(2)}) copy-start(f32[2048,64]{0,1:T(8,128)S(1)} %broadcast_divide_fusion) | copy-start | bytes 1572868
  255.0 67.3 %copy-start.1 = (f32[2048,64]{0,1:T(8,128)S(1)}, f32[2048,64]{0,1:T(8,128)}, u32[]{:S(2)}) copy-start(f32[2048,64]{0,1:T(8,128)} %param.8) | copy-start | bytes 1572868
Sparse Core Ops, SparseCore 0:
  48.5 59.2 all-reduce.2
  203.6 35.9 all-reduce.4
where the time goes:
time: 330 us; the launch traced here: 329 us
  matrix products  143 us (43%)
  waiting for transfers between devices  95.5 us (29%)
  blocking collectives  47.8 us (14%)
  other arithmetic  27.1 us (8%)
  between operations  14.2 us (4%)
    psum x1, waiting for transfers between devices, on_device(): left_raw = lax.psum(partial_value, 'col')  59.4 us
    dot_general x1, matrix products, on_device(): jnp.dot(blended, right_factor, precision=HIGH, preferred_element_type=jnp...  40.1 us
    dot_general x1, matrix products, on_device(): jnp.dot(left, right.T, precision=HIGH, preferred_element_type=jnp.float32)  37.9 us
    psum x1, waiting for transfers between devices, on_device(): right = lax.psum(right_part(blended, left), 'row')  36.1 us
    dot_general x1, matrix products, on_device(): jnp.dot(left, normed.T, precision=HIGH, preferred_element_type=jnp.float32)  29.4 us
    dot_general x1, matrix products, right_part(): lax.dot_general(blended, factor, (((0,), (0,)), ((), ())), precision=HIGH...  29.1 us
    psum x1, blocking collectives, on_device(): gram_one = lax.psum(gram_of(left_raw), 'row')  18.8 us
    psum x1, blocking collectives, on_device(): gram_two = lax.psum(gram_of(left_one), 'row')  15.8 us
  transfers between devices with their start and end apart: 2, of which 2 were waited for; matrix products, arithmetic and copies ran while one was open for 0% of the time, Pallas kernels for 0%

commit v1 on v0

v1 whole, which is shorter than its diff:
```python
import functools
import math

import jax
import jax.numpy as jnp
from jax import lax
from jax.experimental import pallas as pl
from jax.experimental.pallas import tpu as pltpu
from jax.sharding import PartitionSpec as P

F32 = jnp.float32
BF16 = jnp.bfloat16
HIGH = lax.Precision.HIGHEST
SLOTS = 5
MIB = 1024 * 1024


def dot_high(a, b, dims):
    return lax.dot_general(a, b, (dims, ((), ())), precision=HIGH, preferred_element_type=F32)


def dot_bf16(a, b):
    return lax.dot_general(a, b, (((1,), (0,)), ((), ())), preferred_element_type=F32)


def halves(x):
    high = x.astype(BF16)
    return high, (x - high.astype(F32)).astype(BF16)


def eliminate(gram):
    rank = gram.shape[0]
    rows = lax.broadcasted_iota(jnp.int32, (rank, rank), 0)
    cols = lax.broadcasted_iota(jnp.int32, (rank, rank), 1)
    eye = jnp.where(rows == cols, 1.0, 0.0).astype(F32)
    wide = jnp.concatenate([gram, eye], axis=1)
    at = lax.broadcasted_iota(jnp.int32, (rank, 1), 0)
    root = jnp.zeros((rank, 1), F32)
    for j in range(rank):
        column = wide[:, j : j + 1]
        pivot = wide[j : j + 1, j : j + 1]
        row = wide[j : j + 1, :] * (1.0 / pivot)
        root = jnp.where(at == j, lax.rsqrt(pivot), root)
        wide = wide - jnp.where(at > j, column, 0.0) * row
    wide = wide * root
    upper = jnp.where(cols >= rows, wide[:, :rank], 0.0)
    return upper, wide[:, rank:]


class Exchange:
    def __init__(self, axis, count, local, slots, send, recv):
        self.axis, self.count = axis, count
        self.local, self.slots, self.send, self.recv = local, slots, send, recv
        self.me = lax.axis_index(axis)

    def copy(self, step, peer, slot):
        return pltpu.make_async_remote_copy(
            src_ref=self.local,
            dst_ref=self.slots.at[slot],
            send_sem=self.send.at[step],
            recv_sem=self.recv.at[slot],
            device_id={self.axis: peer},
            device_id_type=pl.DeviceIdType.MESH,
        )

    def start(self, value):
        self.local[...] = value
        self.slots[self.me] = value
        for step in range(1, self.count):
            self.copy(step, lax.rem(self.me + step, self.count), self.me).start()

    def finish(self):
        for step in range(1, self.count):
            peer = lax.rem(self.me + step, self.count)
            self.copy(step, peer, peer).wait()
        total = self.slots[0]
        for step in range(1, self.count):
            total = total + self.slots[step]
        return total


class AllReduce:
    def __init__(self, axis, count, rank, acc, full, boxes, send, recv):
        self.axis, self.acc, self.full, self.boxes = axis, acc, full, boxes
        self.send, self.recv = send, recv
        me = lax.axis_index(axis)
        offset, size = 0, rank
        self.stages = []
        for bit in range(count.bit_length() - 1):
            one = lax.rem(me // (1 << bit), 2)
            peer = me + (1 - 2 * one) * (1 << bit)
            halve = size >= 16
            if halve:
                half = size // 2
                keep, give = offset + one * half, offset + (1 - one) * half
            else:
                half, keep, give = size, offset, offset
            self.stages.append((peer, halve, half, keep, give))
            offset, size = keep, half
        self.offset, self.size = offset, size
        self.back = [s for s in reversed(range(len(self.stages))) if self.stages[s][1]]
        self.steps = len(self.stages) + len(self.back)

    def rows(self, start, size):
        return pl.ds(start if isinstance(start, int) else pl.multiple_of(start, 8), size)

    def copy(self, step, block, cols):
        n = len(self.stages)
        if step < n:
            peer, halve, half, keep, give = self.stages[step]
            src = self.acc.at[self.rows(give, half), cols]
            dst = self.boxes[step].at[:, cols]
        else:
            peer, halve, half, keep, give = self.stages[self.back[step - n]]
            src = self.full.at[self.rows(keep, half), cols]
            dst = self.full.at[self.rows(keep, half), cols]
        return pltpu.make_async_remote_copy(
            src_ref=src,
            dst_ref=dst,
            send_sem=self.send.at[step, block],
            recv_sem=self.recv.at[step, block],
            device_id={self.axis: peer},
            device_id_type=pl.DeviceIdType.MESH,
        )

    def start(self, step, block, cols):
        self.copy(step, block, cols).start()

    def finish(self, step, block, cols):
        self.copy(step, block, cols).wait()
        n = len(self.stages)
        if step < n:
            half, keep = self.stages[step][2:4]
            kept = self.rows(keep, half)
            self.acc[kept, cols] = self.acc[kept, cols] + self.boxes[step][:, cols]
            if step == n - 1:
                own = self.rows(self.offset, self.size)
                self.full[own, cols] = self.acc[own, cols]
        if step + 1 < self.steps:
            self.start(step + 1, block, cols)


def box_rows(count, rank):
    sizes, size = [], rank
    for _ in range(count.bit_length() - 1):
        if size >= 16:
            size //= 2
        sizes.append(size)
    return sizes


def step_count(count, rank):
    size, steps = rank, 0
    for _ in range(count.bit_length() - 1):
        steps += 1
        if size >= 16:
            size //= 2
            steps += 1
    return steps


def factor_kernel(plan, mom, grad, rf, yt, linv, rt, nt, first, *refs):
    m, n, rank, nr, nc, tile, chunk, group = plan
    refs = list(refs)
    take = lambda count: [refs.pop(0) for _ in range(count)]
    (bh, bm, mbuf, gbuf, rp, acc, full, yp, wacc, wfull, qs, us) = take(12)
    boxes_y = take(nc.bit_length() - 1)
    boxes_w = take(nr.bit_length() - 1)
    ex = [take(4) for _ in range(3)]
    (in_sem, ysend, yrecv, wsend, wrecv) = take(5)

    tiles, chunks, per = m // tile, m // chunk, chunk // tile
    slots = min(SLOTS, tiles)

    def load(t, slot):
        src = pl.ds(pl.multiple_of(t * tile, tile), tile)
        return (
            pltpu.make_async_copy(mom.at[src, :], mbuf.at[slot], in_sem.at[0, slot]),
            pltpu.make_async_copy(grad.at[src, :], gbuf.at[slot], in_sem.at[1, slot]),
        )

    for t in range(slots):
        for c in load(t, t):
            c.start()

    barrier = pltpu.get_barrier_semaphore()
    row, col = lax.axis_index("row"), lax.axis_index("col")
    for step in range(1, nc):
        pl.semaphore_signal(
            barrier, inc=1, device_id={"col": lax.rem(col + step, nc)}, device_id_type=pl.DeviceIdType.MESH
        )
    for step in range(1, nr):
        pl.semaphore_signal(
            barrier, inc=1, device_id={"row": lax.rem(row + step, nr)}, device_id_type=pl.DeviceIdType.MESH
        )

    r = rf[...]
    r_high, r_rest = halves(r)
    r_mid, r_low = halves(r - r_high.astype(F32))
    rp[:, :rank] = r_high
    rp[:, rank : 2 * rank] = r_mid
    rp[:, 2 * rank :] = r_low
    gram_r = dot_high(r, r, ((0,), (0,)))

    pl.semaphore_wait(barrier, nc + nr - 2)

    ex_r = Exchange("col", nc, *ex[0])
    ex_g = Exchange("row", nr, *ex[1])
    ex_s = Exchange("col", nc, *ex[2])
    sum_y = AllReduce("col", nc, rank, acc, full, boxes_y, ysend, yrecv)
    sum_w = AllReduce("row", nr, rank, wacc, wfull, boxes_w, wsend, wrecv)

    ex_r.start(gram_r)

    def chunk_cols(c):
        return pl.ds(pl.multiple_of(c * chunk, chunk), chunk)

    def body(c, carry):
        for step in reversed(range(sum_y.steps)):
            old = c - step - 1

            @pl.when((old >= 0) & (old < chunks))
            def _(step=step, old=old):
                sum_y.finish(step, old, chunk_cols(old))

        @pl.when(c < chunks)
        def _():
            for k in range(per):
                t = c * per + k
                slot = lax.rem(t, slots)
                for copy in load(t, slot):
                    copy.wait()
                blended = mbuf[slot] + gbuf[slot].astype(F32)
                high, low = halves(blended)
                here = pl.ds(pl.multiple_of(t * tile, tile), tile)
                bh[here, :] = high
                bm[here, :] = low
                part = dot_bf16(high, rp[...]) + dot_bf16(low, rp[...])
                part = part.T
                part = part[:rank] + (part[rank : 2 * rank] + part[2 * rank :])
                acc[:, here] = part

                @pl.when(t + slots < tiles)
                def _():
                    for copy in load(t + slots, slot):
                        copy.start()

            sum_y.start(0, c, chunk_cols(c))

        @pl.when(c == min(2, chunks - 1))
        def _():
            g = ex_r.finish()
            rows = lax.broadcasted_iota(jnp.int32, (rank, rank), 0)
            cols = lax.broadcasted_iota(jnp.int32, (rank, rank), 1)
            diag = jnp.where(rows == cols, g, 0.0)
            trace = jnp.sum(jnp.sum(diag, axis=1, keepdims=True), axis=0, keepdims=True)
            g = g + jnp.where(rows == cols, trace * (2.0**-22), 0.0)
            upper, inverse = eliminate(g)
            us[...] = upper
            qs[...] = inverse

        return carry

    lax.fori_loop(0, chunks + sum_y.steps, body, 0)

    q = qs[...]

    def whiten(c, gram):
        cols = chunk_cols(c)
        y = dot_high(q, full[:, cols], ((1,), (0,)))
        yt[:, cols] = y
        high, low = halves(y)
        yp[:rank, cols] = high
        yp[rank:, cols] = low
        return gram + dot_high(y, y, ((1,), (1,)))

    gram_y = lax.fori_loop(0, chunks, whiten, jnp.zeros((rank, rank), F32))
    ex_g.start(gram_y)

    groups = n // group
    sub = min(256, group)

    def group_cols(g):
        return pl.ds(g * group, group)

    for g in range(groups):

        def right_part(s, carry):
            cols = pl.ds(pl.multiple_of(g * group + s * sub, sub), sub)
            w = dot_bf16(yp[...], bh[:, cols]) + dot_bf16(yp[...], bm[:, cols])
            wacc[:, cols] = w[:rank] + w[rank:]
            return carry

        lax.fori_loop(0, group // sub, right_part, 0)
        sum_w.start(0, g, group_cols(g))

    g_all = ex_g.finish()
    upper, inverse = eliminate(g_all)
    first[...] = dot_high(us[...], upper, ((0,), (1,))) * (1.0 / math.sqrt(float(m * nr) * float(n * nc)))
    for g in range(groups):
        sum_w.finish(0, g, group_cols(g))
    g_two = dot_high(dot_high(inverse, g_all, ((1,), (0,))), inverse, ((1,), (1,)))
    _, inverse_two = eliminate(g_two)
    both = dot_high(inverse_two, inverse, ((1,), (0,)))
    linv[...] = both
    for step in range(1, sum_w.steps):
        for g in range(groups):
            sum_w.finish(step, g, group_cols(g))
    squares = jnp.zeros((rank, 1), F32)
    for g in range(groups):
        right = dot_high(both, wfull[:, group_cols(g)], ((1,), (0,)))
        rt[:, group_cols(g)] = right
        squares = squares + jnp.sum(right * right, axis=1, keepdims=True)
    ex_s.start(jnp.broadcast_to(squares, (rank, 128)))
    norms = jnp.sqrt(ex_s.finish()[:, :1]) + 1e-06
    nt[...] = rt[...] * (1.0 / norms)


def factors(plan, momentum, gradient, right_factor):
    m, n, rank, nr, nc, tile, chunk, group = plan
    slots = min(SLOTS, m // tile)
    vmem = pltpu.VMEM
    dma = pltpu.SemaphoreType.DMA

    def exchange(count, width):
        return [vmem((rank, width), F32), vmem((count, rank, width), F32), dma((count,)), dma((count,))]

    scratch = [
        vmem((m, n), BF16),
        vmem((m, n), BF16),
        vmem((slots, tile, n), F32),
        vmem((slots, tile, n), BF16),
        vmem((n, 3 * rank), BF16),
        vmem((rank, m), F32),
        vmem((rank, m), F32),
        vmem((2 * rank, m), BF16),
        vmem((rank, n), F32),
        vmem((rank, n), F32),
        vmem((rank, rank), F32),
        vmem((rank, rank), F32),
    ]
    scratch += [vmem((rows, m), F32) for rows in box_rows(nc, rank)]
    scratch += [vmem((rows, n), F32) for rows in box_rows(nr, rank)]
    scratch += exchange(nc, rank) + exchange(nr, rank) + exchange(nc, 128)
    steps_y, steps_w = step_count(nc, rank), step_count(nr, rank)
    scratch += [
        dma((2, slots)),
        dma((steps_y, m // chunk)),
        dma((steps_y, m // chunk)),
        dma((steps_w, n // group)),
        dma((steps_w, n // group)),
    ]
    whole = pl.BlockSpec(memory_space=vmem)
    return pl.pallas_call(
        functools.partial(factor_kernel, plan),
        out_shape=[
            jax.ShapeDtypeStruct((rank, m), F32),
            jax.ShapeDtypeStruct((rank, rank), F32),
            jax.ShapeDtypeStruct((rank, n), F32),
            jax.ShapeDtypeStruct((rank, n), F32),
            jax.ShapeDtypeStruct((rank, rank), F32),
        ],
        in_specs=[pl.BlockSpec(memory_space=pl.ANY), pl.BlockSpec(memory_space=pl.ANY), whole],
        out_specs=[whole] * 5,
        scratch_shapes=scratch,
        compiler_params=pltpu.CompilerParams(
            collective_id=0, has_side_effects=True, vmem_limit_bytes=60 * MIB
        ),
        name="factors",
    )(momentum, gradient, right_factor)


def output_kernel(scale, rank, mom, grad, yt, linv, rt, nt, first, update, left, normed, new, first_out, rhs_u, rhs_m):
    @pl.when(pl.program_id(0) == 0)
    def _():
        normed_t = nt[...]
        normed[...] = normed_t.T
        first_out[...] = first[...]
        for ref, value in ((rhs_u, normed_t * scale), (rhs_m, rt[...] * 0.05)):
            high, low = halves(value)
            for k in range(2):
                ref[2 * k * rank : (2 * k + 1) * rank, :] = high
                ref[(2 * k + 1) * rank : (2 * k + 2) * rank, :] = low

    lt = dot_high(linv[...], yt[...], ((1,), (0,)))
    left[...] = lt.T
    high = lt.astype(BF16).astype(F32)
    low = lt - high
    lhs = jnp.concatenate([high, high, low, low], axis=0).T.astype(BF16)
    update[...] = dot_bf16(lhs, rhs_u[...]).astype(BF16)
    new[...] = (mom[...] + grad[...].astype(F32)) - dot_bf16(lhs, rhs_m[...])


def outputs(scale, tile, momentum, gradient, yt, linv, rt, nt, first):
    m, n = momentum.shape
    rank = linv.shape[0]
    fixed = lambda shape: pl.BlockSpec(shape, lambda i: (0, 0))
    rows = lambda width: pl.BlockSpec((tile, width), lambda i: (i, 0))
    return pl.pallas_call(
        functools.partial(output_kernel, scale, rank),
        grid=(m // tile,),
        out_shape=[
            jax.ShapeDtypeStruct((m, n), BF16),
            jax.ShapeDtypeStruct((m, rank), F32),
            jax.ShapeDtypeStruct((n, rank), F32),
            jax.ShapeDtypeStruct((m, n), F32),
            jax.ShapeDtypeStruct((rank, rank), F32),
        ],
        in_specs=[
            rows(n),
            rows(n),
            pl.BlockSpec((rank, tile), lambda i: (0, i)),
            fixed((rank, rank)),
            fixed((rank, n)),
            fixed((rank, n)),
            fixed((rank, rank)),
        ],
        out_specs=[rows(n), rows(rank), fixed((n, rank)), rows(n), fixed((rank, rank))],
        scratch_shapes=[pltpu.VMEM((4 * rank, n), BF16), pltpu.VMEM((4 * rank, n), BF16)],
        compiler_params=pltpu.CompilerParams(vmem_limit_bytes=40 * MIB),
        name="outputs",
    )(momentum, gradient, yt, linv, rt, nt, first)


def on_device(nr, nc, momentum, gradient, right_factor):
    m, n = momentum.shape
    rank = right_factor.shape[1]
    tile = min(128, m)
    chunk = min(512, m)
    group = min(1024, n)
    plan = (m, n, rank, nr, nc, tile, chunk, group)
    scale = math.sqrt(float(m * nr) * float(n * nc) / float(rank))
    yt, linv, rt, nt, first = factors(plan, momentum, gradient, right_factor)
    return tuple(outputs(scale, tile, momentum, gradient, yt, linv, rt, nt, first))


def solution(mesh):
    in_specs = (P("row", "col"), P("row", "col"), P("col", None))
    out_specs = (P("row", "col"), P("row", None), P("col", None), P("row", "col"), P())
    return jax.shard_map(
        functools.partial(on_device, mesh.shape["row"], mesh.shape["col"]),
        mesh=mesh,
        in_specs=in_specs,
        out_specs=out_specs,
        check_vma=False,
    )
```

time: 330 us -> 163 us (0.49)
  Pallas kernels: 0 us -> 152 us
  matrix products: 143 us -> 0 us
  waiting for transfers between devices: 95.5 us -> 0 us
  blocking collectives: 47.8 us -> 0 us
  other arithmetic: 27.1 us -> 0 us
  between operations: 14.2 us -> 0.65 us
  local copies, waits for them, and re-layouts: 1.16 us -> 9.84 us
    pallas_call x0 -> x2, Pallas kernels: none -> 152 us  [the longest x1 102 us: factors(): pl.pallas_call(functools.partial(factor_kernel, plan), out_shape=[jax.Sha...]
    dot_general x6 -> x0, matrix products: 140 us -> none  [the longest x1 40.1 us: on_device(): jnp.dot(blended, right_factor, precision=HIGH, preferred_element_type=jnp...]
    psum x2 -> x0, waiting for transfers between devices: 95.5 us -> none  [the longest x1 59.4 us: on_device(): left_raw = lax.psum(partial_value, 'col')]
    psum x3 -> x0, blocking collectives: 47.8 us -> none  [the longest x1 18.8 us: on_device(): gram_one = lax.psum(gram_of(left_raw), 'row')]
    another operation x9 -> x0, other arithmetic: 23.5 us -> none  [the longest x3 10.4 us: apply_lower(): lax.linalg.triangular_solve(lower, block, left_side=False, lower=True, tr...]
    unnamed x8 -> x11, local copies, waits for them, and re-layouts: 1.02 us -> 7.17 us
    another operation x2 -> x0, matrix products: 3.32 us -> none  [apply_lower(): lax.linalg.triangular_solve(lower, block, left_side=False, lower=True, tr...]
  transfers between devices with their start and end apart: 2 -> 0, of which waited for: 2 -> 0; matrix products, arithmetic and copies ran while one was open for 0% -> 0% of each run, Pallas kernels for 0% -> 0%
where the time goes in v1:
time: 163 us; the launch traced here: 162 us
  Pallas kernels  152 us (93%)
  local copies, waits for them, and re-layouts  9.84 us (6%)
    pallas_call x1, Pallas kernels, factors(): pl.pallas_call(functools.partial(factor_kernel, plan), out_shape=[jax.Sha...  102 us
    pallas_call x1, Pallas kernels, outputs(): pl.pallas_call(functools.partial(output_kernel, scale, rank), grid=(m //...  50.1 us
    unnamed x11, local copies, waits for them, and re-layouts  7.17 us

profile of v1, /device:TPU:0, one launch (start us, length us, event | category | flops | bytes accessed | tf_op | source)
XLA Modules:
  0.0 162.4 jit_solution(12775476245234704083)
XLA Ops:
  0.6 2.4 %copy.8.rf = f32[2048,64]{1,0:T(8,128)} copy(f32[2048,64]{0,1:T(8,128)} %param.5) | data formatting | bytes 1048576 | tf_op args[2]
  3.0 101.7 %factors.1 = (f32[64,4096]{1,0:T(8,128)}, f32[64,64]{1,0:T(8,128)}, f32[64,2048]{1,0:T(8,128)}, f32[64,2048]{1,0:T(8,128)}, f32[64,64]{1,0:T(8,128)}) custom-call(f32[4096,2048]{1,0:T(8,128)} %mom.3, bf16[4096,2048]{1,0:T(8,128)(2,1)} %grad.3, f32[2048,64]{1,0:T(8,128)} %copy.8.rf), custom_call_target="tpu_custom_call" | custom-call | tf_op jit(solution)/shard_map/factors/pallas_call | solution.py:354
  104.7 0.0 copy-start
  104.7 1.2 copy-done
  106.0 0.0 copy-start.1
  106.0 1.0 copy-done.1
  107.0 0.0 copy-start.2
  107.0 1.0 copy-done.2
  108.0 0.0 copy-start.3
  108.0 0.8 copy-done.3
  108.8 0.0 copy-start.4
  108.8 0.8 copy-done.4
  109.6 50.1 %outputs.1 = (bf16[4096,2048]{1,0:T(8,128)(2,1)}, f32[4096,64]{1,0:T(8,128)S(1)}, f32[2048,64]{1,0:T(8,128)S(1)}, f32[4096,2048]{1,0:T(8,128)}, f32[64,64]{1,0:T(8,128)}) custom-call(f32[4096,2048]{1,0:T(8,128)} %mom.3, bf16[4096,2048]{1,0:T(8,128)(2,1)} %grad.3, f32[64,4096]{1,0:T(8,128)S(1)} %copy-done, f32[64,64]{1,0:T(8,128)S(1)} %copy-done.3, ...), custom_call_target="tpu_custom_call" | custom-call | tf_op jit(solution)/shard_map/outputs/pallas_call | solution.py:399
  159.7 1.1 copy.10
  160.8 1.6 copy.9
Async XLA Ops:
  104.7 1.2 copy-start
  106.0 1.0 copy-start.1
  107.0 1.0 copy-start.2
  108.0 0.8 copy-start.3
  108.8 0.8 copy-start.4

commit v2 on v1

--- a/solution.py
+++ b/solution.py
@@ -28,23 +28,35 @@
     return high, (x - high.astype(F32)).astype(BF16)
 
 
-def eliminate(gram):
+def widen(gram):
     rank = gram.shape[0]
     rows = lax.broadcasted_iota(jnp.int32, (rank, rank), 0)
     cols = lax.broadcasted_iota(jnp.int32, (rank, rank), 1)
-    eye = jnp.where(rows == cols, 1.0, 0.0).astype(F32)
-    wide = jnp.concatenate([gram, eye], axis=1)
-    at = lax.broadcasted_iota(jnp.int32, (rank, 1), 0)
-    root = jnp.zeros((rank, 1), F32)
-    for j in range(rank):
+    return jnp.concatenate([gram, jnp.where(rows == cols, 1.0, 0.0).astype(F32)], axis=1)
+
+
+def eliminate_columns(wide, root, columns):
+    at = lax.broadcasted_iota(jnp.int32, (wide.shape[0], 1), 0)
+    for j in columns:
         column = wide[:, j : j + 1]
         pivot = wide[j : j + 1, j : j + 1]
         row = wide[j : j + 1, :] * (1.0 / pivot)
         root = jnp.where(at == j, lax.rsqrt(pivot), root)
         wide = wide - jnp.where(at > j, column, 0.0) * row
+    return wide, root
+
+
+def split_factors(wide, root):
+    rank = wide.shape[0]
+    rows = lax.broadcasted_iota(jnp.int32, (rank, rank), 0)
+    cols = lax.broadcasted_iota(jnp.int32, (rank, rank), 1)
     wide = wide * root
-    upper = jnp.where(cols >= rows, wide[:, :rank], 0.0)
-    return upper, wide[:, rank:]
+    return jnp.where(cols >= rows, wide[:, :rank], 0.0), wide[:, rank:]
+
+
+def eliminate(gram):
+    rank = gram.shape[0]
+    return split_factors(*eliminate_columns(widen(gram), jnp.zeros((rank, 1), F32), range(rank)))
 
 
 class Exchange:
@@ -159,17 +171,18 @@
     return steps
 
 
-def factor_kernel(plan, mom, grad, rf, yt, linv, rt, nt, first, *refs):
+def factor_kernel(plan, mom, grad, rf, lhs, lt, rt, nt, first, *refs):
     m, n, rank, nr, nc, tile, chunk, group = plan
     refs = list(refs)
     take = lambda count: [refs.pop(0) for _ in range(count)]
-    (bh, bm, mbuf, gbuf, rp, acc, full, yp, wacc, wfull, qs, us) = take(12)
+    (bh, bm, mbuf, gbuf, rp, acc, full, yp, ws, rs) = take(10)
     boxes_y = take(nc.bit_length() - 1)
     boxes_w = take(nr.bit_length() - 1)
     ex = [take(4) for _ in range(3)]
     (in_sem, ysend, yrecv, wsend, wrecv) = take(5)
 
     tiles, chunks, per = m // tile, m // chunk, chunk // tile
+    pair = min(2, per)
     slots = min(SLOTS, tiles)
 
     def load(t, slot):
@@ -197,10 +210,9 @@
     r = rf[...]
     r_high, r_rest = halves(r)
     r_mid, r_low = halves(r - r_high.astype(F32))
-    rp[:, :rank] = r_high
-    rp[:, rank : 2 * rank] = r_mid
-    rp[:, 2 * rank :] = r_low
-    gram_r = dot_high(r, r, ((0,), (0,)))
+    pieces = jnp.concatenate([p.astype(F32) for p in (r_high, r_mid, r_low)], axis=0)
+    rp[...] = pieces.T.astype(BF16)
+    gram_r = dot_high(r, r, ((1,), (1,)))
 
     pl.semaphore_wait(barrier, nc + nr - 2)
 
@@ -208,7 +220,7 @@
     ex_g = Exchange("row", nr, *ex[1])
     ex_s = Exchange("col", nc, *ex[2])
     sum_y = AllReduce("col", nc, rank, acc, full, boxes_y, ysend, yrecv)
-    sum_w = AllReduce("row", nr, rank, wacc, wfull, boxes_w, wsend, wrecv)
+    sum_w = AllReduce("row", nr, rank, acc, full, boxes_w, wsend, wrecv)
 
     ex_r.start(gram_r)
 
@@ -225,50 +237,59 @@
 
         @pl.when(c < chunks)
         def _():
-            for k in range(per):
-                t = c * per + k
-                slot = lax.rem(t, slots)
-                for copy in load(t, slot):
-                    copy.wait()
-                blended = mbuf[slot] + gbuf[slot].astype(F32)
-                high, low = halves(blended)
-                here = pl.ds(pl.multiple_of(t * tile, tile), tile)
-                bh[here, :] = high
-                bm[here, :] = low
-                part = dot_bf16(high, rp[...]) + dot_bf16(low, rp[...])
-                part = part.T
-                part = part[:rank] + (part[rank : 2 * rank] + part[2 * rank :])
-                acc[:, here] = part
-
-                @pl.when(t + slots < tiles)
-                def _():
-                    for copy in load(t + slots, slot):
-                        copy.start()
+            for k in range(0, per, pair):
+                for t in range(pair):
+                    t = c * per + k + t
+                    slot = lax.rem(t, slots)
+                    for copy in load(t, slot):
+                        copy.wait()
+                    high, low = halves(mbuf[slot] + gbuf[slot].astype(F32))
+                    here = pl.ds(pl.multiple_of(t * tile, tile), tile)
+                    bh[here, :] = high
+                    bm[here, :] = low
+
+                    @pl.when(t + slots < tiles)
+                    def _(t=t, slot=slot):
+                        for copy in load(t + slots, slot):
+                            copy.start()
+
+                here = pl.ds(pl.multiple_of((c * per + k) * tile, pair * tile), pair * tile)
+                both = jnp.concatenate([bh[here, :], bm[here, :]], axis=0)
+                part = dot_bf16(both, rp[...])
+                part = (part[: pair * tile] + part[pair * tile :]).T
+                acc[:, here] = part[:rank] + (part[rank : 2 * rank] + part[2 * rank :])
 
             sum_y.start(0, c, chunk_cols(c))
 
-        @pl.when(c == min(2, chunks - 1))
+        @pl.when(c == chunks)
         def _():
             g = ex_r.finish()
             rows = lax.broadcasted_iota(jnp.int32, (rank, rank), 0)
             cols = lax.broadcasted_iota(jnp.int32, (rank, rank), 1)
             diag = jnp.where(rows == cols, g, 0.0)
             trace = jnp.sum(jnp.sum(diag, axis=1, keepdims=True), axis=0, keepdims=True)
-            g = g + jnp.where(rows == cols, trace * (2.0**-22), 0.0)
-            upper, inverse = eliminate(g)
-            us[...] = upper
-            qs[...] = inverse
+            ws[...] = widen(g + jnp.where(rows == cols, trace * (2.0**-22), 0.0))
+            rs[...] = jnp.zeros((rank, 1), F32)
+
+        for k in range(4):
+
+            @pl.when(c == chunks + min(k, sum_y.steps - 1))
+            def _(k=k):
+                wide, root = eliminate_columns(
+                    ws[...], rs[...], range(k * rank // 4, (k + 1) * rank // 4)
+                )
+                ws[...] = wide
+                rs[...] = root
 
         return carry
 
     lax.fori_loop(0, chunks + sum_y.steps, body, 0)
-
-    q = qs[...]
+    upper_r, q = split_factors(ws[...], rs[...])
 
     def whiten(c, gram):
         cols = chunk_cols(c)
         y = dot_high(q, full[:, cols], ((1,), (0,)))
-        yt[:, cols] = y
+        lt[:, cols] = y
         high, low = halves(y)
         yp[:rank, cols] = high
         yp[rank:, cols] = low
@@ -283,32 +304,47 @@
     def group_cols(g):
         return pl.ds(g * group, group)
 
-    for g in range(groups):
-
-        def right_part(s, carry):
+    def right_part(g):
+        def one(s, carry):
             cols = pl.ds(pl.multiple_of(g * group + s * sub, sub), sub)
             w = dot_bf16(yp[...], bh[:, cols]) + dot_bf16(yp[...], bm[:, cols])
-            wacc[:, cols] = w[:rank] + w[rank:]
+            acc[:, cols] = w[:rank] + w[rank:]
             return carry
 
-        lax.fori_loop(0, group // sub, right_part, 0)
+        lax.fori_loop(0, group // sub, one, 0)
         sum_w.start(0, g, group_cols(g))
 
-    g_all = ex_g.finish()
-    upper, inverse = eliminate(g_all)
-    first[...] = dot_high(us[...], upper, ((0,), (1,))) * (1.0 / math.sqrt(float(m * nr) * float(n * nc)))
-    for g in range(groups):
-        sum_w.finish(0, g, group_cols(g))
-    g_two = dot_high(dot_high(inverse, g_all, ((1,), (0,))), inverse, ((1,), (1,)))
-    _, inverse_two = eliminate(g_two)
-    both = dot_high(inverse_two, inverse, ((1,), (0,)))
-    linv[...] = both
-    for step in range(1, sum_w.steps):
-        for g in range(groups):
-            sum_w.finish(step, g, group_cols(g))
+    def left_part(c, carry):
+        cols = chunk_cols(c)
+        left_t = dot_high(both, lt[:, cols], ((1,), (0,)))
+        lt[:, cols] = left_t
+        high = left_t.astype(BF16).astype(F32)
+        low = left_t - high
+        lhs[cols, :] = jnp.concatenate([high, high, low, low], axis=0).T.astype(BF16)
+        return carry
+
+    for i in range(groups + max(sum_w.steps, 3)):
+        for step in reversed(range(sum_w.steps)):
+            if 0 <= i - 1 - step < groups:
+                sum_w.finish(step, i - 1 - step, group_cols(i - 1 - step))
+        if i < groups:
+            right_part(i)
+        if i == groups:
+            g_all = ex_g.finish()
+            upper, inverse = eliminate(g_all)
+            first[...] = dot_high(upper_r, upper, ((0,), (1,))) * (
+                1.0 / math.sqrt(float(m * nr) * float(n * nc))
+            )
+        if i == groups + 1:
+            g_two = dot_high(dot_high(inverse, g_all, ((1,), (0,))), inverse, ((1,), (1,)))
+            _, inverse_two = eliminate(g_two)
+            both = dot_high(inverse_two, inverse, ((1,), (0,)))
+        if i == groups + 2:
+            lax.fori_loop(0, chunks, left_part, 0)
+
     squares = jnp.zeros((rank, 1), F32)
     for g in range(groups):
-        right = dot_high(both, wfull[:, group_cols(g)], ((1,), (0,)))
+        right = dot_high(both, full[:, group_cols(g)], ((1,), (0,)))
         rt[:, group_cols(g)] = right
         squares = squares + jnp.sum(right * right, axis=1, keepdims=True)
     ex_s.start(jnp.broadcast_to(squares, (rank, 128)))
@@ -331,13 +367,11 @@
         vmem((slots, tile, n), F32),
         vmem((slots, tile, n), BF16),
         vmem((n, 3 * rank), BF16),
-        vmem((rank, m), F32),
-        vmem((rank, m), F32),
+        vmem((rank, max(m, n)), F32),
+        vmem((rank, max(m, n)), F32),
         vmem((2 * rank, m), BF16),
-        vmem((rank, n), F32),
-        vmem((rank, n), F32),
-        vmem((rank, rank), F32),
-        vmem((rank, rank), F32),
+        vmem((rank, 2 * rank), F32),
+        vmem((rank, 1), F32),
     ]
     scratch += [vmem((rows, m), F32) for rows in box_rows(nc, rank)]
     scratch += [vmem((rows, n), F32) for rows in box_rows(nr, rank)]
@@ -354,8 +388,8 @@
     return pl.pallas_call(
         functools.partial(factor_kernel, plan),
         out_shape=[
+            jax.ShapeDtypeStruct((m, 4 * rank), BF16),
             jax.ShapeDtypeStruct((rank, m), F32),
-            jax.ShapeDtypeStruct((rank, rank), F32),
             jax.ShapeDtypeStruct((rank, n), F32),
             jax.ShapeDtypeStruct((rank, n), F32),
             jax.ShapeDtypeStruct((rank, rank), F32),
@@ -370,56 +404,57 @@
     )(momentum, gradient, right_factor)
 
 
-def output_kernel(scale, rank, mom, grad, yt, linv, rt, nt, first, update, left, normed, new, first_out, rhs_u, rhs_m):
+def output_kernel(scale, rank, mom, grad, lhs, lt, rt, nt, first, update, left, normed, new, first_out, rhs_u, rhs_m):
+    tile, n = mom.shape
+
     @pl.when(pl.program_id(0) == 0)
     def _():
-        normed_t = nt[...]
-        normed[...] = normed_t.T
+        normed[...] = nt[...]
         first_out[...] = first[...]
-        for ref, value in ((rhs_u, normed_t * scale), (rhs_m, rt[...] * 0.05)):
+        for ref, value in ((rhs_u, nt[...] * scale), (rhs_m, rt[...] * 0.05)):
             high, low = halves(value)
             for k in range(2):
                 ref[2 * k * rank : (2 * k + 1) * rank, :] = high
                 ref[(2 * k + 1) * rank : (2 * k + 2) * rank, :] = low
 
-    lt = dot_high(linv[...], yt[...], ((1,), (0,)))
-    left[...] = lt.T
-    high = lt.astype(BF16).astype(F32)
-    low = lt - high
-    lhs = jnp.concatenate([high, high, low, low], axis=0).T.astype(BF16)
-    update[...] = dot_bf16(lhs, rhs_u[...]).astype(BF16)
-    new[...] = (mom[...] + grad[...].astype(F32)) - dot_bf16(lhs, rhs_m[...])
-
-
-def outputs(scale, tile, momentum, gradient, yt, linv, rt, nt, first):
+    here = pl.ds(pl.multiple_of(pl.program_id(0) * tile, tile), tile)
+    left[...] = lt[:, here]
+    rows = lhs[here, :]
+    width = min(256, n)
+    for at in range(0, n, width):
+        cols = pl.ds(at, width)
+        update[:, cols] = dot_bf16(rows, rhs_u[:, cols]).astype(BF16)
+        new[:, cols] = (mom[:, cols] + grad[:, cols].astype(F32)) - dot_bf16(rows, rhs_m[:, cols])
+
+
+def outputs(scale, tile, momentum, gradient, lhs, lt, rt, nt, first):
     m, n = momentum.shape
-    rank = linv.shape[0]
+    rank = lt.shape[0]
     fixed = lambda shape: pl.BlockSpec(shape, lambda i: (0, 0))
     rows = lambda width: pl.BlockSpec((tile, width), lambda i: (i, 0))
+    whole = pl.BlockSpec(memory_space=pltpu.VMEM)
     return pl.pallas_call(
         functools.partial(output_kernel, scale, rank),
         grid=(m // tile,),
         out_shape=[
             jax.ShapeDtypeStruct((m, n), BF16),
-            jax.ShapeDtypeStruct((m, rank), F32),
-            jax.ShapeDtypeStruct((n, rank), F32),
+            jax.ShapeDtypeStruct((rank, m), F32),
+            jax.ShapeDtypeStruct((rank, n), F32),
             jax.ShapeDtypeStruct((m, n), F32),
             jax.ShapeDtypeStruct((rank, rank), F32),
         ],
-        in_specs=[
-            rows(n),
+        in_specs=[rows(n), rows(n)] + [whole] * 5,
+        out_specs=[
             rows(n),
             pl.BlockSpec((rank, tile), lambda i: (0, i)),
-            fixed((rank, rank)),
             fixed((rank, n)),
-            fixed((rank, n)),
+            rows(n),
             fixed((rank, rank)),
         ],
-        out_specs=[rows(n), rows(rank), fixed((n, rank)), rows(n), fixed((rank, rank))],
         scratch_shapes=[pltpu.VMEM((4 * rank, n), BF16), pltpu.VMEM((4 * rank, n), BF16)],
         compiler_params=pltpu.CompilerParams(vmem_limit_bytes=40 * MIB),
         name="outputs",
-    )(momentum, gradient, yt, linv, rt, nt, first)
+    )(momentum, gradient, lhs, lt, rt, nt, first)
 
 
 def on_device(nr, nc, momentum, gradient, right_factor):
@@ -427,11 +462,14 @@
     rank = right_factor.shape[1]
     tile = min(128, m)
     chunk = min(512, m)
-    group = min(1024, n)
+    group = min(512, n)
     plan = (m, n, rank, nr, nc, tile, chunk, group)
     scale = math.sqrt(float(m * nr) * float(n * nc) / float(rank))
-    yt, linv, rt, nt, first = factors(plan, momentum, gradient, right_factor)
-    return tuple(outputs(scale, tile, momentum, gradient, yt, linv, rt, nt, first))
+    lhs, lt, rt, nt, first = factors(plan, momentum, gradient, right_factor.T)
+    update, left, normed, new, first = outputs(
+        scale, min(256, m), momentum, gradient, lhs, lt, rt, nt, first
+    )
+    return update, left.T, normed.T, new, first
 
 
 def solution(mesh):

time: 163 us -> 157 us (0.963)
  local copies, waits for them, and re-layouts: 9.84 us -> 5.65 us
  Pallas kernels: 152 us -> 150 us
    pallas_call x1, Pallas kernels: 50.1 us -> 39.9 us  [outputs(): pl.pallas_call(functools.partial(output_kernel, scale, rank), grid=(m //...]
    pallas_call x1, Pallas kernels: 102 us -> 110 us  [factors(): pl.pallas_call(functools.partial(factor_kernel, plan), out_shape=[jax.Sha...]
    pallas_call x2 -> x0, local copies, waits for them, and re-layouts: 2.67 us -> none  [outputs(): pl.pallas_call(functools.partial(output_kernel, scale, rank), grid=(m //...]
    unnamed x11 -> x10, local copies, waits for them, and re-layouts: 7.17 us -> 5.65 us
where the time goes in v2:
time: 157 us; the launch traced here: 156 us
  Pallas kernels  150 us (96%)
  local copies, waits for them, and re-layouts  5.65 us (4%)
    pallas_call x1, Pallas kernels, factors(): pl.pallas_call(functools.partial(factor_kernel, plan), out_shape=[jax.Sha...  110 us
    pallas_call x1, Pallas kernels, outputs(): pl.pallas_call(functools.partial(output_kernel, scale, rank), grid=(m //...  39.9 us
    unnamed x10, local copies, waits for them, and re-layouts  5.65 us

profile of v2, /device:TPU:0, one launch (start us, length us, event | category | flops | bytes accessed | tf_op | source)
XLA Modules:
  0.0 156.5 jit_solution(18419324809097614447)
XLA Ops:
  0.6 110.2 %factors.1 = (bf16[4096,256]{1,0:T(8,128)(2,1)}, f32[64,4096]{1,0:T(8,128)}, f32[64,2048]{1,0:T(8,128)}, f32[64,2048]{1,0:T(8,128)}, f32[64,64]{1,0:T(8,128)}) custom-call(f32[4096,2048]{1,0:T(8,128)} %mom.3, bf16[4096,2048]{1,0:T(8,128)(2,1)} %grad.3, f32[64,2048]{1,0:T(8,128)} %bitcast.3), custom_call_target="tpu_custom_call" | custom-call | tf_op jit(solution)/shard_map/factors/pallas_call | solution.py:388
  110.9 0.0 copy-start
  110.9 1.6 %copy-done = bf16[4096,256]{1,0:T(8,128)(2,1)S(1)} copy-done((bf16[4096,256]{1,0:T(8,128)(2,1)S(1)}, bf16[4096,256]{1,0:T(8,128)(2,1)}, u32[]{:S(2)}) %copy-start) | copy-done | bytes 2097176
  112.5 0.0 copy-start.1
  112.5 1.2 copy-done.1
  113.7 0.0 copy-start.2
  113.7 1.0 copy-done.2
  114.7 0.0 copy-start.3
  114.7 1.0 copy-done.3
  115.8 0.0 copy-start.4
  115.8 0.8 copy-done.4
  116.5 39.9 %outputs.1 = (bf16[4096,2048]{1,0:T(8,128)(2,1)}, f32[64,4096]{1,0:T(8,128)}, f32[64,2048]{1,0:T(8,128)}, f32[4096,2048]{1,0:T(8,128)}, f32[64,64]{1,0:T(8,128)}) custom-call(f32[4096,2048]{1,0:T(8,128)} %mom.3, bf16[4096,2048]{1,0:T(8,128)(2,1)} %grad.3, bf16[4096,256]{1,0:T(8,128)(2,1)S(1)} %copy-done, f32[64,4096]{1,0:T(8,128)S(1)} %copy-done.1, ...), custom_call_target="tpu_custom_call" | custom-call | tf_op jit(solution)/shard_map/outputs/pallas_call | solution.py:436
Async XLA Ops:
  110.9 1.6 %copy-start = (bf16[4096,256]{1,0:T(8,128)(2,1)S(1)}, bf16[4096,256]{1,0:T(8,128)(2,1)}, u32[]{:S(2)}) copy-start(bf16[4096,256]{1,0:T(8,128)(2,1)} %get-tuple-element.15.lhs) | copy-start | bytes 6291460
  112.5 1.2 copy-start.1
  113.7 1.0 copy-start.2
  114.7 1.0 copy-start.3
  115.8 0.8 copy-start.4

commit v3 on v2

--- a/solution.py
+++ b/solution.py
@@ -35,28 +35,41 @@
     return jnp.concatenate([gram, jnp.where(rows == cols, 1.0, 0.0).astype(F32)], axis=1)
 
 
-def eliminate_columns(wide, root, columns):
-    at = lax.broadcasted_iota(jnp.int32, (wide.shape[0], 1), 0)
-    for j in columns:
-        column = wide[:, j : j + 1]
-        pivot = wide[j : j + 1, j : j + 1]
-        row = wide[j : j + 1, :] * (1.0 / pivot)
-        root = jnp.where(at == j, lax.rsqrt(pivot), root)
-        wide = wide - jnp.where(at > j, column, 0.0) * row
-    return wide, root
-
-
-def split_factors(wide, root):
+def eliminate_columns(wide, columns):
+    rank, lanes = wide.shape
+    at = lax.broadcasted_iota(jnp.int32, (8, lanes), 0)
+    blocks = [wide[k : k + 8, :] for k in range(0, rank, 8)]
+    for j in range(columns[0], columns[-1] + 1, 4):
+        top = j // 8
+        spread = [
+            {k: jnp.broadcast_to(blocks[k][:, j + a : j + a + 1], (8, lanes)) for k in range(top, rank // 8)}
+            for a in range(4)
+        ]
+        for a in range(4):
+            here = j + a - 8 * top
+            inverse = 1.0 / spread[a][top][here : here + 1, :]
+            lows = dict(spread[a])
+            lows[top] = jnp.where(at > here, lows[top], 0.0)
+            for b in range(a + 1, 4):
+                entry = spread[b][top][here : here + 1, :] * inverse
+                spread[b] = {k: spread[b][k] - lows[k] * entry for k in lows}
+            row = blocks[top][here : here + 1, :] * inverse
+            for k in lows:
+                blocks[k] = blocks[k] - lows[k] * row
+    return jnp.concatenate(blocks, axis=0)
+
+
+def split_factors(wide):
     rank = wide.shape[0]
     rows = lax.broadcasted_iota(jnp.int32, (rank, rank), 0)
     cols = lax.broadcasted_iota(jnp.int32, (rank, rank), 1)
-    wide = wide * root
+    pivots = jnp.sum(jnp.where(rows == cols, wide[:, :rank], 0.0), axis=1, keepdims=True)
+    wide = wide * (1.0 / jnp.sqrt(pivots))
     return jnp.where(cols >= rows, wide[:, :rank], 0.0), wide[:, rank:]
 
 
 def eliminate(gram):
-    rank = gram.shape[0]
-    return split_factors(*eliminate_columns(widen(gram), jnp.zeros((rank, 1), F32), range(rank)))
+    return split_factors(eliminate_columns(widen(gram), range(gram.shape[0])))
 
 
 class Exchange:
@@ -171,15 +184,15 @@
     return steps
 
 
-def factor_kernel(plan, mom, grad, rf, lhs, lt, rt, nt, first, *refs):
+def factor_kernel(plan, mom, grad, rf, lhs_out, lt_out, rt_out, nt_out, first_out, *refs):
     m, n, rank, nr, nc, tile, chunk, group = plan
     refs = list(refs)
     take = lambda count: [refs.pop(0) for _ in range(count)]
-    (bh, bm, mbuf, gbuf, rp, acc, full, yp, ws, rs) = take(10)
+    (bh, bm, mbuf, gbuf, rp, acc, full, yp, ws, lt, first) = take(11)
     boxes_y = take(nc.bit_length() - 1)
     boxes_w = take(nr.bit_length() - 1)
     ex = [take(4) for _ in range(3)]
-    (in_sem, ysend, yrecv, wsend, wrecv) = take(5)
+    (in_sem, out_sem, lhs_sem, ysend, yrecv, wsend, wrecv) = take(7)
 
     tiles, chunks, per = m // tile, m // chunk, chunk // tile
     pair = min(2, per)
@@ -269,22 +282,17 @@
             diag = jnp.where(rows == cols, g, 0.0)
             trace = jnp.sum(jnp.sum(diag, axis=1, keepdims=True), axis=0, keepdims=True)
             ws[...] = widen(g + jnp.where(rows == cols, trace * (2.0**-22), 0.0))
-            rs[...] = jnp.zeros((rank, 1), F32)
 
         for k in range(4):
 
             @pl.when(c == chunks + min(k, sum_y.steps - 1))
             def _(k=k):
-                wide, root = eliminate_columns(
-                    ws[...], rs[...], range(k * rank // 4, (k + 1) * rank // 4)
-                )
-                ws[...] = wide
-                rs[...] = root
+                ws[...] = eliminate_columns(ws[...], range(k * rank // 4, (k + 1) * rank // 4))
 
         return carry
 
     lax.fori_loop(0, chunks + sum_y.steps, body, 0)
-    upper_r, q = split_factors(ws[...], rs[...])
+    upper_r, q = split_factors(ws[...])
 
     def whiten(c, gram):
         cols = chunk_cols(c)
@@ -314,14 +322,35 @@
         lax.fori_loop(0, group // sub, one, 0)
         sum_w.start(0, g, group_cols(g))
 
-    def left_part(c, carry):
-        cols = chunk_cols(c)
+    across = n // (4 * rank)
+
+    def lhs_copy(t):
+        lanes = pl.ds(pl.multiple_of(lax.rem(t, across) * 4 * rank, 4 * rank), 4 * rank)
+        rows = pl.ds(pl.multiple_of(t * tile, tile), tile)
+        return pltpu.make_async_copy(gbuf.at[t // across, :, lanes], lhs_out.at[rows, :], lhs_sem.at[t])
+
+    def left_part(t, carry):
+        cols = pl.ds(pl.multiple_of(t * tile, tile), tile)
         left_t = dot_high(both, lt[:, cols], ((1,), (0,)))
         lt[:, cols] = left_t
         high = left_t.astype(BF16).astype(F32)
         low = left_t - high
-        lhs[cols, :] = jnp.concatenate([high, high, low, low], axis=0).T.astype(BF16)
+        lanes = pl.ds(pl.multiple_of(lax.rem(t, across) * 4 * rank, 4 * rank), 4 * rank)
+        gbuf[t // across, :, lanes] = jnp.concatenate([high, high, low, low], axis=0).T.astype(BF16)
+        lhs_copy(t).start()
         return carry
+
+    def lhs_end(t, carry):
+        lhs_copy(t).wait()
+        return carry
+
+    def out(k, src, dst):
+        return pltpu.make_async_copy(src, dst, out_sem.at[k])
+
+    lt_copy = out(0, lt, lt_out)
+    rt_copy = out(1, acc.at[:, pl.ds(0, n)], rt_out)
+    nt_copy = out(2, full.at[:, pl.ds(0, n)], nt_out)
+    first_copy = out(3, first, first_out)
 
     for i in range(groups + max(sum_w.steps, 3)):
         for step in reversed(range(sum_w.steps)):
@@ -340,16 +369,23 @@
             _, inverse_two = eliminate(g_two)
             both = dot_high(inverse_two, inverse, ((1,), (0,)))
         if i == groups + 2:
-            lax.fori_loop(0, chunks, left_part, 0)
+            lax.fori_loop(0, tiles, left_part, 0)
+            lt_copy.start()
+            first_copy.start()
 
     squares = jnp.zeros((rank, 1), F32)
     for g in range(groups):
         right = dot_high(both, full[:, group_cols(g)], ((1,), (0,)))
-        rt[:, group_cols(g)] = right
+        acc[:, group_cols(g)] = right
         squares = squares + jnp.sum(right * right, axis=1, keepdims=True)
+    rt_copy.start()
     ex_s.start(jnp.broadcast_to(squares, (rank, 128)))
     norms = jnp.sqrt(ex_s.finish()[:, :1]) + 1e-06
-    nt[...] = rt[...] * (1.0 / norms)
+    full[:, :n] = acc[:, :n] * (1.0 / norms)
+    nt_copy.start()
+    lax.fori_loop(0, tiles, lhs_end, 0)
+    for copy in (lt_copy, rt_copy, nt_copy, first_copy):
+        copy.wait()
 
 
 def factors(plan, momentum, gradient, right_factor):
@@ -371,7 +407,8 @@
         vmem((rank, max(m, n)), F32),
         vmem((2 * rank, m), BF16),
         vmem((rank, 2 * rank), F32),
-        vmem((rank, 1), F32),
+        vmem((rank, m), F32),
+        vmem((rank, rank), F32),
     ]
     scratch += [vmem((rows, m), F32) for rows in box_rows(nc, rank)]
     scratch += [vmem((rows, n), F32) for rows in box_rows(nr, rank)]
@@ -379,6 +416,8 @@
     steps_y, steps_w = step_count(nc, rank), step_count(nr, rank)
     scratch += [
         dma((2, slots)),
+        dma((4,)),
+        dma((m // tile,)),
         dma((steps_y, m // chunk)),
         dma((steps_y, m // chunk)),
         dma((steps_w, n // group)),
@@ -395,7 +434,7 @@
             jax.ShapeDtypeStruct((rank, rank), F32),
         ],
         in_specs=[pl.BlockSpec(memory_space=pl.ANY), pl.BlockSpec(memory_space=pl.ANY), whole],
-        out_specs=[whole] * 5,
+        out_specs=[pl.BlockSpec(memory_space=pl.ANY)] * 5,
         scratch_shapes=scratch,
         compiler_params=pltpu.CompilerParams(
             collective_id=0, has_side_effects=True, vmem_limit_bytes=60 * MIB
@@ -417,9 +456,8 @@
                 ref[2 * k * rank : (2 * k + 1) * rank, :] = high
                 ref[(2 * k + 1) * rank : (2 * k + 2) * rank, :] = low
 
-    here = pl.ds(pl.multiple_of(pl.program_id(0) * tile, tile), tile)
-    left[...] = lt[:, here]
-    rows = lhs[here, :]
+    left[...] = lt[...]
+    rows = lhs[...]
     width = min(256, n)
     for at in range(0, n, width):
         cols = pl.ds(at, width)
@@ -432,7 +470,6 @@
     rank = lt.shape[0]
     fixed = lambda shape: pl.BlockSpec(shape, lambda i: (0, 0))
     rows = lambda width: pl.BlockSpec((tile, width), lambda i: (i, 0))
-    whole = pl.BlockSpec(memory_space=pltpu.VMEM)
     return pl.pallas_call(
         functools.partial(output_kernel, scale, rank),
         grid=(m // tile,),
@@ -443,7 +480,15 @@
             jax.ShapeDtypeStruct((m, n), F32),
             jax.ShapeDtypeStruct((rank, rank), F32),
         ],
-        in_specs=[rows(n), rows(n)] + [whole] * 5,
+        in_specs=[
+            rows(n),
+            rows(n),
+            rows(4 * rank),
+            pl.BlockSpec((rank, tile), lambda i: (0, i)),
+            fixed((rank, n)),
+            fixed((rank, n)),
+            fixed((rank, rank)),
+        ],
         out_specs=[
             rows(n),
             pl.BlockSpec((rank, tile), lambda i: (0, i)),
@@ -452,7 +497,7 @@
             fixed((rank, rank)),
         ],
         scratch_shapes=[pltpu.VMEM((4 * rank, n), BF16), pltpu.VMEM((4 * rank, n), BF16)],
-        compiler_params=pltpu.CompilerParams(vmem_limit_bytes=40 * MIB),
+        compiler_params=pltpu.CompilerParams(vmem_limit_bytes=60 * MIB),
         name="outputs",
     )(momentum, gradient, lhs, lt, rt, nt, first)
 
@@ -467,7 +512,7 @@
     scale = math.sqrt(float(m * nr) * float(n * nc) / float(rank))
     lhs, lt, rt, nt, first = factors(plan, momentum, gradient, right_factor.T)
     update, left, normed, new, first = outputs(
-        scale, min(256, m), momentum, gradient, lhs, lt, rt, nt, first
+        scale, min(512, m), momentum, gradient, lhs, lt, rt, nt, first
     )
     return update, left.T, normed.T, new, first
 

time: 157 us -> 146 us (0.930)
  local copies, waits for them, and re-layouts: 5.65 us -> 0 us
  Pallas kernels: 150 us -> 145 us
    unnamed x10 -> x0, local copies, waits for them, and re-layouts: 5.65 us -> none
    pallas_call x1, Pallas kernels: 39.9 us -> 36.1 us  [outputs(): pl.pallas_call(functools.partial(output_kernel, scale, rank), grid=(m //...]
where the time goes in v3:
time: 146 us; the launch traced here: 145 us
  Pallas kernels  145 us (99%)
    pallas_call x1, Pallas kernels, factors(): pl.pallas_call(functools.partial(factor_kernel, plan), out_shape=[jax.Sha...  109 us
    pallas_call x1, Pallas kernels, outputs(): pl.pallas_call(functools.partial(output_kernel, scale, rank), grid=(m //...  36.1 us

profile of v3, /device:TPU:0, one launch (start us, length us, event | category | flops | bytes accessed | tf_op | source)
XLA Modules:
  0.0 145.4 jit_solution(7919891487206491054)
XLA Ops:
  0.6 108.7 %factors.1 = (bf16[4096,256]{1,0:T(8,128)(2,1)}, f32[64,4096]{1,0:T(8,128)}, f32[64,2048]{1,0:T(8,128)}, f32[64,2048]{1,0:T(8,128)}, f32[64,64]{1,0:T(8,128)}) custom-call(f32[4096,2048]{1,0:T(8,128)} %mom.3, bf16[4096,2048]{1,0:T(8,128)(2,1)} %grad.3, f32[64,2048]{1,0:T(8,128)} %bitcast.3), custom_call_target="tpu_custom_call" | custom-call | tf_op jit(solution)/shard_map/factors/pallas_call | solution.py:427
  109.3 36.1 %outputs.1 = (bf16[4096,2048]{1,0:T(8,128)(2,1)}, f32[64,4096]{1,0:T(8,128)}, f32[64,2048]{1,0:T(8,128)}, f32[4096,2048]{1,0:T(8,128)}, f32[64,64]{1,0:T(8,128)}) custom-call(f32[4096,2048]{1,0:T(8,128)} %mom.3, bf16[4096,2048]{1,0:T(8,128)(2,1)} %grad.3, bf16[4096,256]{1,0:T(8,128)(2,1)} %get-tuple-element.15.lhs, f32[64,4096]{1,0:T(8,128)} %get-tuple-element.16.lt, ...), custom_call_target="tpu_custom_call" | custom-call | tf_op jit(solution)/shard_map/outputs/pallas_call | solution.py:473
